TPU v7x, 512 devices: a whole 4x8x8 slice. The times are simulated.
512 devices in a mesh: seq: 128 (over y, z, core), fsdp: 4 (over x).
Axes of the slice: x: 4, y: 8, z: 8, core: 2. Of those that a mesh axis runs over, the one named last changes fastest.
Arguments:
- tokens: bfloat16 [4, 16384, 2048], P('fsdp', 'seq'), may hold values from -14 to 14
- w_qkv: bfloat16 [2048, 3, 1024], P(None, None, 'fsdp'), may hold values from -0.125 to 0.125
- w_feature: bfloat16 [8, 128, 16], replicated, may hold values from -2 to 2
- norm_gain: float32 [1024], replicated, may hold values from 0.5 to 1.5
- log_decay: float32 [4, 8, 16384], P('fsdp', None, 'seq'), may hold values from -1.5 to 0
- pattern: int32 [4, 256, 3], P('fsdp', 'seq'), may hold values from 1 to 255, as said below
Outputs:
- mixed: bfloat16 [4, 16384, 1024], P('fsdp', 'seq')
Inputs may be any that keep to these rules, and one draw needn't show every extreme that they name: `pattern`: the 3 blocks of query block b are distinct, none is among the first 1 block or equal to b - 1, b or b + 1, and each lies in a segment at most 3 segments from b's segment; the first lies exactly 3 segments later where that segment exists, else 3 segments earlier.
All inputs are finite; a program needn't handle non-finite values.
Results may differ from a plain program's by a relative error of at most 0.0097.
The roundings to bfloat16 on the way count: a program that leaves them out, or rounds other values in their place, can miss the bound.
Values may be sent and summed in bfloat16 or wider, within the bound.
No kernel may reach another device: no remote copies, remote signals or barrier semaphores. Data moves between devices by JAX's collectives and lax.ppermute only.
A program may use at most 64 MiB of HBM per device.

v0:
```python
import jax
import jax.numpy as jnp
from jax import lax
from jax.sharding import PartitionSpec as P

HALF_HEADS = 8
DH = 128
F = 16
HD = 1024
BS = 64
G = 1
R = 3
RD = 3
TOK_DEV = 128
NB_DEV = 2
epsilon = 1e-06
masked_score = -1e30


def from_behind(value, axis, steps):
    count = lax.axis_size(axis)
    initial, last = (max(0, -steps), min(count, count - steps))
    return lax.ppermute(value, axis, [(source, source + steps) for source in range(initial, last)])


def spread(array, axis, root):
    mine = lax.axis_index(axis) == root
    return lax.psum(jnp.where(mine, array, jnp.zeros_like(array)), axis)


def entering(value, axis, join, neutral):
    count, mine = (lax.axis_size(axis), lax.axis_index(axis))
    pieces = jax.tree.map(lambda part: lax.all_gather(part, axis), value)
    running = jax.tree.map(
        lambda part, zero: jnp.full_like(part, 0) + jnp.asarray(zero, part.dtype), value, neutral
    )

    def lap(position, running):
        longer = join(running, jax.tree.map(lambda part: part[position], pieces))
        return jax.tree.map(lambda new, old: jnp.where(position < mine, new, old), longer, running)

    return lax.fori_loop(0, count - 1, lap, running)


def feature_map(projected_head, w_feature):
    logits = jnp.einsum(
        "thd,hdf->htf", projected_head, w_feature, preferred_element_type=jnp.float32
    )
    return jax.nn.softmax(logits, axis=-1).astype(jnp.bfloat16)


def combine_states(earlier, following):
    return (earlier[0] * following[0], following[0][:, None, None] * earlier[1] + following[1])


def neighbour_piece(pair_rows, offset):
    return from_behind(pair_rows, "seq", -offset)


def per_device(tokens, w_qkv, w_feature, norm_gain, log_decay, pattern):
    projected = jnp.einsum(
        "btd,dkc->btkc",
        tokens,
        lax.all_gather(w_qkv, "fsdp", axis=2, tiled=True),
        preferred_element_type=jnp.float32,
    ).astype(jnp.bfloat16)
    queries = projected[0, :, 0].reshape(TOK_DEV, HALF_HEADS, DH)
    key_rows = projected[0, :, 1].reshape(TOK_DEV, HALF_HEADS, DH)
    values = projected[0, :, 2].reshape(TOK_DEV, HALF_HEADS, DH)
    pair_rows = projected[:, :, 1:3].reshape(1, TOK_DEV, 2 * HD)
    pieces = []
    for offset in range(-RD, RD + 1):
        if offset == 0:
            pieces.append(pair_rows)
        else:
            pieces.append(neighbour_piece(pair_rows, offset))
    region = jnp.concatenate(pieces, axis=1)
    global_rows = spread(pair_rows[0, : G * BS], "seq", 0)
    phi_query = feature_map(queries, w_feature)
    phi_key = feature_map(key_rows, w_feature)
    log_steps = log_decay[0]
    cumulative = jnp.cumsum(log_steps, axis=1)
    final_log = cumulative[:, -1:]
    weighted_key = (
        jnp.exp(final_log - cumulative)[:, :, None] * phi_key.astype(jnp.float32)
    ).astype(jnp.bfloat16)
    local_state = jnp.einsum(
        "htf,thd->hfd", weighted_key, values, preferred_element_type=jnp.float32
    )
    identity = (jnp.ones((HALF_HEADS,), jnp.float32), jnp.zeros((HALF_HEADS, F, DH), jnp.float32))
    carried_pair = entering(
        (jnp.exp(final_log[:, 0]), local_state), "seq", combine_states, identity
    )
    carried = carried_pair[1]
    scores = jnp.einsum("htf,hsf->hts", phi_query, phi_key, preferred_element_type=jnp.float32)
    log_gap = cumulative[:, :, None] - cumulative[:, None, :]
    causal = jnp.arange(TOK_DEV)[:, None] >= jnp.arange(TOK_DEV)[None, :]
    decay_matrix = jnp.where(causal[None], jnp.exp(jnp.minimum(log_gap, 0.0)), 0.0)
    mixing = (scores * decay_matrix).astype(jnp.bfloat16)
    local_term = jnp.einsum("hts,shd->thd", mixing, values, preferred_element_type=jnp.float32)
    carried_term = jnp.einsum(
        "htf,hfd->thd", phi_query.astype(jnp.float32), carried, precision=lax.Precision.HIGHEST
    )
    carried_term = carried_term * jnp.exp(cumulative).T[:, :, None]
    linear = local_term + carried_term
    normed = linear * lax.rsqrt(jnp.mean(linear * linear, axis=-1, keepdims=True) + epsilon)
    normed = normed * norm_gain.reshape(HALF_HEADS, DH)
    device = lax.axis_index("seq")
    block_total = lax.axis_size("seq") * NB_DEV
    window_blocks = region[0].reshape((2 * RD + 1) * NB_DEV, BS, 2 * HD)
    query_blocks = device * NB_DEV + jnp.arange(NB_DEV, dtype=jnp.int32)
    near_blocks = query_blocks[:, None] + jnp.arange(-1, 2, dtype=jnp.int32)[None, :]
    usable_near = (near_blocks >= G) & (near_blocks < block_total)
    chosen = jnp.concatenate([near_blocks, pattern[0]], axis=1) - (device - RD) * NB_DEV
    chosen = jnp.clip(chosen, 0, (2 * RD + 1) * NB_DEV - 1)
    usable = jnp.concatenate([usable_near, jnp.ones((NB_DEV, R), dtype=bool)], axis=1)
    usable_keys = jnp.repeat(usable, BS, axis=1)
    picked = jnp.take(window_blocks, chosen, axis=0).reshape(
        NB_DEV, (3 + R) * BS, 2, HALF_HEADS, DH
    )
    global_split = global_rows.reshape(G * BS, 2, HALF_HEADS, DH)
    query_rows = queries.reshape(NB_DEV, BS, HALF_HEADS, DH)
    score_scale = DH ** (-0.5)
    near_scores = (
        jnp.einsum(
            "nqhd,nkhd->nhqk", query_rows, picked[:, :, 0], preferred_element_type=jnp.float32
        )
        * score_scale
    )
    near_scores = jnp.where(usable_keys[:, None, None, :], near_scores, masked_score)
    far_scores = (
        jnp.einsum(
            "nqhd,khd->nhqk", query_rows, global_split[:, 0], preferred_element_type=jnp.float32
        )
        * score_scale
    )
    scores_all = jnp.concatenate([near_scores, far_scores], axis=-1)
    highest = jnp.max(scores_all, axis=-1, keepdims=True)
    exponent = jnp.exp(scores_all - highest)
    denominator = jnp.sum(exponent, axis=-1, keepdims=True)
    soft_weights = (exponent / denominator).astype(jnp.bfloat16)
    near_count = (3 + R) * BS
    sparse = jnp.einsum(
        "nhqk,nkhd->nqhd",
        soft_weights[..., :near_count],
        picked[:, :, 1],
        preferred_element_type=jnp.float32,
    )
    sparse = sparse + jnp.einsum(
        "nhqk,khd->nqhd",
        soft_weights[..., near_count:],
        global_split[:, 1],
        preferred_element_type=jnp.float32,
    )
    sparse = sparse.reshape(TOK_DEV, HALF_HEADS, DH)
    return (normed + sparse).astype(jnp.bfloat16).reshape(1, TOK_DEV, HD)


def solution(mesh):
    placed = (
        P("fsdp", "seq", None),
        P(None, None, "fsdp"),
        P(),
        P(),
        P("fsdp", None, "seq"),
        P("fsdp", "seq", None),
    )
    return jax.shard_map(
        per_device, mesh=mesh, in_specs=placed, out_specs=P("fsdp", "seq", None), check_vma=False
    )
```

profile of v0, /device:TPU:9, one launch (start us, length us, event | category | flops | bytes accessed | tf_op | source)
XLA Modules:
  0.0 615.5 jit_solution(8857086100503208488)
XLA Ops:
  7.9 133.5 %all-gather.5.cloned.1.call-done = bf16[2048,3,1024]{2,0,1:T(8,128)(2,1)} async-done(((bf16[2048,3,256]{2,0,1:T(8,128)(2,1)}), bf16[2048,3,1024]{2,0,1:T(8,128)(2,1)}) %all-gather.5.cloned.1.call-update) | async-done | bytes 12582928 | tf_op jit(solution)/shard_map/all_gather | solution.py:64
  141.4 6.4 %fusion.7 = bf16[1,128,3,1024]{3,1,2,0:T(8,128)(2,1)S(1)} fusion(bf16[2048,3,1024]{2,0,1:T(8,128)(2,1)} %all-gather.5.cloned.1.call-done, bf16[1,128,2048]{2,1,0:T(8,128)(2,1)S(1)} %copy-done), kind=kOutput, calls=%fused_computation.17 | convolution fusion | flops 1611005952 | bytes 13893632 | tf_op jit(solution)/shard_map/btd,dkc->btkc/dot_general | solution.py:61
  151.9 1.3 dynamic-slice
  154.0 213.7 %all-reduce.1 = f32[1024]{0:T(1024)S(1)} all-reduce(f32[1024]{0:T(1024)S(1)} %dynamic-update-slice), channel_id=2, replica_groups=mesh['seq'=128,'fsdp'=4] {'seq'}, use_global_device_ids=true, to_apply=%add.1 | all-reduce | flops 1024 | bytes 8192
  368.4 1.9 collective-permute-start
  370.3 1.9 collective-permute-start.1
  372.3 2.1 collective-permute-start.2
  374.3 5.9 collective-permute-start.3
  380.2 7.2 %collective-permute-start.4 = (bf16[1,128,2048]{1,2,0:T(8,128)(2,1)S(1)}, bf16[1,128,2048]{1,2,0:T(8,128)(2,1)S(1)}, u32[]{:S(2)}, u32[]{:S(2)}) collective-permute-start(bf16[1,128,2048]{1,2,0:T(8,128)(2,1)S(1)} %bitcast.123), channel_id=1, source_target_pairs={{8,0},{12,4},{16,8},{20,12},{24,16},{28,20},{32,24},{36,28},{40,32... | collective-permute-start | bytes 1572872 | tf_op jit(solution)/shard_map/ppermute | solution.py:23
  388.0 1.1 fusion.37
  389.4 8.5 %collective-permute-done = bf16[1,128,2048]{1,2,0:T(8,128)(2,1)} collective-permute-done((bf16[1,128,2048]{1,2,0:T(8,128)(2,1)S(1)}, bf16[1,128,2048]{1,2,0:T(8,128)(2,1)}, u32[]{:S(2)}, u32[]{:S(2)}) %collective-permute-start) | collective-permute-done | bytes 524320 | tf_op jit(solution)/shard_map/ppermute | solution.py:23
  397.9 3.3 collective-permute-start.5
  401.2 1.9 constant_dynamic-update-slice_fusion.6
  403.1 1.9 constant_dynamic-update-slice_fusion.5
  405.4 1.9 constant_dynamic-update-slice_fusion.4
  408.2 1.0 constant_dynamic-update-slice_fusion.2
  410.1 3.3 collective-permute-done.5
  414.2 6.2 %copy.54 = bf16[1,896,2048]{2,1,0:T(8,128)(2,1)} copy(bf16[1,896,2048]{1,2,0:T(8,128)(2,1)} %constant_dynamic-update-slice_fusion) | data formatting | bytes 7340032 | tf_op jit(solution)/shard_map/concatenate | solution.py:77
  420.4 4.6 gather_fusion
  425.0 2.9 copy.70
  432.0 52.2 %all-gather.7.cloned.1.call-done = f32[1024,16,128]{2,1,0:T(8,128)} async-done(((f32[8,16,128]{2,1,0:T(8,128)}), f32[1024,16,128]{2,1,0:T(8,128)}) %all-gather.7.cloned.1.call-update) | async-done | bytes 8388624 | tf_op jit(solution)/shard_map/all_gather | solution.py:33
  484.2 122.4 %while.14 = (s32[]{:T(128)}, f32[8,16,128]{2,1,0:T(8,128)S(1)}, s32[]{:T(128)}, f32[128,8]{1,0:T(8,128)S(1)}, f32[128,8,16,128]{3,2,1,0:T(8,128)}, /*index=5*/s32[]{:T(128)}, s32[]{:T(128)}) while((s32[]{:T(128)}, f32[8,16,128]{2,1,0:T(8,128)S(1)}, s32[]{:T(128)}, f32[128,8]{1,0:T(8,128)S(1)}, f32[128,8,16,128]{3,2,1,0:T(8,128)}, ...), condition=%wide.region_6.7_spmd.clone, body=%wide.region_5.6_spmd.clone.sunk | while | flops 65540 | bytes 196809 | solution.py:42
  485.2 0.9 fusion.58
  486.1 0.9 fusion.58
  (341 shorter events, 132.9 us)
Async XLA Ops:
  6.5 134.9 %copy-start = (bf16[1,128,2048]{2,1,0:T(8,128)(2,1)S(1)}, bf16[1,128,2048]{2,1,0:T(8,128)(2,1)}, u32[]{:S(2)}) copy-start(bf16[1,128,2048]{2,1,0:T(8,128)(2,1)} %param.8) | copy-start | bytes 1572868
  6.5 0.8 copy-start.6
  6.5 134.9 %all-gather.5.cloned.1.call-start = ((), (), s32[]{:S(2)}) async-start(), calls=%async_computation | async-start | bytes 15728640 | tf_op jit(solution)/shard_map/all_gather | solution.py:64
  7.3 380.8 %all-reduce.4.cloned.1.call-start = ((), (), s32[]{:S(2)}) async-start(), calls=%async_computation.1 | async-start | bytes 524288 | tf_op jit(solution)/shard_map/psum | solution.py:28
  147.8 1.5 copy-start.7
  147.8 2.8 copy-start.5
  149.2 335.0 %all-gather.7.cloned.1.call-start = ((), (), s32[]{:S(2)}) async-start(), calls=%async_computation.2 | async-start | bytes 8454144 | tf_op jit(solution)/shard_map/all_gather | solution.py:33
  149.5 237.9 %copy-start.8 = (f32[8,128,16]{1,2,0:T(8,128)}, f32[8,128,16]{1,2,0:T(8,128)S(1)}, u32[]{:S(2)}) copy-start(f32[8,128,16]{1,2,0:T(8,128)S(1)} %fusion.26) | copy-start | bytes 196612
  149.6 0.9 copy-start.10
  368.4 29.5 %collective-permute-start = (bf16[1,128,2048]{1,2,0:T(8,128)(2,1)S(1)}, bf16[1,128,2048]{1,2,0:T(8,128)(2,1)}, u32[]{:S(2)}, u32[]{:S(2)}) collective-permute-start(bf16[1,128,2048]{1,2,0:T(8,128)(2,1)S(1)} %bitcast.119), channel_id=1, source_target_pairs={{0,12},{4,16},{8,20},{12,24},{16,28},{20,32},{24,36},{28,40},{32,4... | collective-permute-start | bytes 1572872 | tf_op jit(solution)/shard_map/ppermute | solution.py:23
  370.3 32.8 %collective-permute-start.1 = (bf16[1,128,2048]{1,2,0:T(8,128)(2,1)S(1)}, bf16[1,128,2048]{1,2,0:T(8,128)(2,1)}, u32[]{:S(2)}, u32[]{:S(2)}) collective-permute-start(bf16[1,128,2048]{1,2,0:T(8,128)(2,1)S(1)} %bitcast.120), channel_id=1, source_target_pairs={{0,8},{4,12},{8,16},{12,20},{16,24},{20,28},{24,32},{28,36},{32,40... | collective-permute-start | bytes 1572872 | tf_op jit(solution)/shard_map/ppermute | solution.py:23
  372.3 33.1 %collective-permute-start.2 = (bf16[1,128,2048]{1,2,0:T(8,128)(2,1)S(1)}, bf16[1,128,2048]{1,2,0:T(8,128)(2,1)}, u32[]{:S(2)}, u32[]{:S(2)}) collective-permute-start(bf16[1,128,2048]{1,2,0:T(8,128)(2,1)S(1)} %bitcast.121), channel_id=1, source_target_pairs={{0,4},{4,8},{8,12},{12,16},{16,20},{20,24},{24,28},{28,32},{32,36}... | collective-permute-start | bytes 1572872 | tf_op jit(solution)/shard_map/ppermute | solution.py:23
  374.3 33.8 %collective-permute-start.3 = (bf16[1,128,2048]{1,2,0:T(8,128)(2,1)S(1)}, bf16[1,128,2048]{1,2,0:T(8,128)(2,1)S(1)}, u32[]{:S(2)}, u32[]{:S(2)}) collective-permute-start(bf16[1,128,2048]{1,2,0:T(8,128)(2,1)S(1)} %bitcast.122), channel_id=1, source_target_pairs={{4,0},{8,4},{12,8},{16,12},{20,16},{24,20},{28,24},{32,28},{36,32}... | collective-permute-start | bytes 1572872 | tf_op jit(solution)/shard_map/ppermute | solution.py:23
  380.2 28.9 %collective-permute-start.4 = (bf16[1,128,2048]{1,2,0:T(8,128)(2,1)S(1)}, bf16[1,128,2048]{1,2,0:T(8,128)(2,1)S(1)}, u32[]{:S(2)}, u32[]{:S(2)}) collective-permute-start(bf16[1,128,2048]{1,2,0:T(8,128)(2,1)S(1)} %bitcast.123), channel_id=1, source_target_pairs={{8,0},{12,4},{16,8},{20,12},{24,16},{28,20},{32,24},{36,28},{40,32... | collective-permute-start | bytes 1572872 | tf_op jit(solution)/shard_map/ppermute | solution.py:23
  397.9 15.4 %collective-permute-start.5 = (bf16[1,128,2048]{1,2,0:T(8,128)(2,1)S(1)}, bf16[1,128,2048]{1,2,0:T(8,128)(2,1)S(1)}, u32[]{:S(2)}, u32[]{:S(2)}) collective-permute-start(bf16[1,128,2048]{1,2,0:T(8,128)(2,1)S(1)} %bitcast.124), channel_id=1, source_target_pairs={{12,0},{16,4},{20,8},{24,12},{28,16},{32,20},{36,24},{40,28},{44,3... | collective-permute-start | bytes 1572872 | tf_op jit(solution)/shard_map/ppermute | solution.py:23
  427.9 0.8 copy-start.3
  430.3 1.0 copy-start.1
  431.2 176.0 %copy-start.2 = (pred[128,128]{1,0:T(8,128)(4,1)S(1)}, pred[128,128]{1,0:T(8,128)(4,1)}, u32[]{:S(2)}) copy-start(pred[128,128]{1,0:T(8,128)(4,1)} %iota_compare_fusion) | copy-start | bytes 49156
  431.3 176.0 %copy-start.9 = (f32[8,128,16]{1,2,0:T(8,128)S(1)}, f32[8,128,16]{1,2,0:T(8,128)}, u32[]{:S(2)}) copy-start(f32[8,128,16]{1,2,0:T(8,128)} %copy-done.8) | copy-start | bytes 196612
  431.3 176.0 %copy-start.11 = (f32[8,128]{1,0:T(8,128)S(1)}, f32[8,128]{1,0:T(8,128)}, u32[]{:S(2)}) copy-start(f32[8,128]{1,0:T(8,128)} %copy-done.10) | copy-start | bytes 12292
  431.5 176.4 %copy-start.4 = (f32[1024]{0:T(1024)S(1)}, f32[1024]{0:T(1024)}, u32[]{:S(2)}) copy-start(f32[1024]{0:T(1024)} %param.11) | copy-start | bytes 12292
Sparse Core Ops, SparseCore 0:
  9.5 131.8 all-gather.4
  149.3 190.4 all-reduce.3
  342.9 141.2 all-gather.6
where the time goes:
time: 622 us; the launch traced here: 615 us
  blocking collectives  214 us (34%)
  waiting for transfers between devices  199 us (32%)
  other arithmetic  121 us (19%)
  local copies, waits for them, and re-layouts  30.1 us (5%)
  starting transfers between devices  22.4 us (4%)
  between operations  14.2 us (2%)
  matrix products  11.5 us (2%)
    unnamed x1, blocking collectives  214 us
    all_gather x1, waiting for transfers between devices, per_device(): lax.all_gather(w_qkv, 'fsdp', axis=2, tiled=True)  134 us
    select_n x127, other arithmetic, lap(): jnp.where(position < mine, new, old)  117 us
    all_gather x1, waiting for transfers between devices, entering(): pieces = jax.tree.map(lambda part: lax.all_gather(part, axis), value)  52.2 us
    ppermute x6, starting transfers between devices, from_behind(): lax.ppermute(value, axis, [(source, source + steps) for source in range(i...  22.3 us
    unnamed x38, local copies, waits for them, and re-layouts  13.2 us
  transfers between devices with their start and end apart: 9, of which 5 were waited for; matrix products, arithmetic and copies ran while one was open for 6% of the time, Pallas kernels for 0%

commit v1 on v0

--- a/solution.py
+++ b/solution.py
@@ -58,11 +58,28 @@
 
 
 def per_device(tokens, w_qkv, w_feature, norm_gain, log_decay, pattern):
+
+    def do_types(local_values, dim_k):
+        cores_n = jax.lax.axis_size("fsdp")
+        fresh = map(lambda b: (b, (b + 1) % cores_n), range(cores_n))
+        val = map(lambda b: (b, (b - 1) % cores_n), range(cores_n))
+        log = list(fresh)
+        parts_seen = list(val)
+        upper, left_arr = ([local_values], [local_values])
+        for _ in range(cores_n // 2):
+            upper.append(jax.lax.ppermute(upper[-1], axis_name="fsdp", perm=log))
+        u = 0
+        while u < (cores_n - 1) // 2:
+            right_arr = jax.lax.ppermute(left_arr[-1], axis_name="fsdp", perm=parts_seen)
+            left_arr.append(right_arr)
+            u = u + 1
+        now = jnp.concatenate([*upper[::-1], *left_arr[1:]], axis=dim_k)
+        return jnp.roll(
+            now, (jax.lax.axis_index("fsdp") - cores_n // 2) * local_values.shape[dim_k], axis=dim_k
+        )
+
     projected = jnp.einsum(
-        "btd,dkc->btkc",
-        tokens,
-        lax.all_gather(w_qkv, "fsdp", axis=2, tiled=True),
-        preferred_element_type=jnp.float32,
+        "btd,dkc->btkc", tokens, do_types(w_qkv, dim_k=2), preferred_element_type=jnp.float32
     ).astype(jnp.bfloat16)
     queries = projected[0, :, 0].reshape(TOK_DEV, HALF_HEADS, DH)
     key_rows = projected[0, :, 1].reshape(TOK_DEV, HALF_HEADS, DH)

time: 622 us -> 739 us (1.19)
  the two profiles are of different devices: /device:TPU:9 before, /device:TPU:1 now
where the time goes in v1:
time: 739 us; the launch traced here: 728 us
  blocking collectives  258 us (35%)
  waiting for transfers between devices  165 us (22%)
  local copies, waits for them, and re-layouts  129 us (17%)
  other arithmetic  122 us (17%)
  starting transfers between devices  27.6 us (4%)
  between operations  14.6 us (2%)
  matrix products  9.19 us (1%)
    unnamed x1, blocking collectives  258 us
    ppermute x2, waiting for transfers between devices, do_types(): upper.append(jax.lax.ppermute(upper[-1], axis_name='fsdp', perm=log))  127 us
    select_n x127, other arithmetic, lap(): jnp.where(position < mine, new, old)  117 us
    mul x127, local copies, waits for them, and re-layouts, combine_states(): following[0][:, None, None] * earlier[1] + following[1]  87.2 us
    unnamed x58, local copies, waits for them, and re-layouts  28.4 us
    all_gather x1, waiting for transfers between devices, entering(): pieces = jax.tree.map(lambda part: lax.all_gather(part, axis), value)  21.2 us
    ppermute x6, waiting for transfers between devices, from_behind(): lax.ppermute(value, axis, [(source, source + steps) for source in range(i...  17.5 us
  transfers between devices with their start and end apart: 11, of which 6 were waited for; matrix products, arithmetic and copies ran while one was open for 5% of the time, Pallas kernels for 0%

profile of v1, /device:TPU:1, one launch (start us, length us, event | category | flops | bytes accessed | tf_op | source)
XLA Modules:
  0.0 728.1 jit_solution(8804246705211678694)
XLA Ops:
  6.5 4.8 copy.47
  11.3 3.9 collective-permute-start
  15.2 63.5 %collective-permute-done = bf16[2048,3,256]{0,2,1:T(8,128)(2,1)} collective-permute-done((bf16[2048,3,256]{0,2,1:T(8,128)(2,1)}, bf16[2048,3,256]{0,2,1:T(8,128)(2,1)}, u32[]{:S(2)}, u32[]{:S(2)}) %collective-permute-start) | collective-permute-done | bytes 3145760 | tf_op jit(solution)/shard_map/ppermute | solution.py:70
  78.7 6.7 collective-permute-start.1
  85.4 4.2 collective-permute-start.2
  90.2 63.2 %collective-permute-done.1 = bf16[2048,3,256]{0,2,1:T(8,128)(2,1)} collective-permute-done((bf16[2048,3,256]{0,2,1:T(8,128)(2,1)}, bf16[2048,3,256]{0,2,1:T(8,128)(2,1)}, u32[]{:S(2)}, u32[]{:S(2)}) %collective-permute-start.1) | collective-permute-done | bytes 3145760 | tf_op jit(solution)/shard_map/ppermute | solution.py:70
  153.4 2.3 constant_dynamic-update-slice_fusion.7
  155.7 2.4 constant_dynamic-update-slice_fusion.6
  158.9 2.3 constant_dynamic-update-slice_fusion.4
  161.2 2.3 constant_dynamic-update-slice_fusion.3
  163.5 2.3 constant_dynamic-update-slice_fusion.2
  166.2 2.3 constant_dynamic-update-slice_fusion
  168.6 3.5 fusion.12
  178.4 258.2 %all-reduce.1 = f32[1024]{0:T(1024)S(1)} all-reduce(f32[1024]{0:T(1024)S(1)} %dynamic-update-slice), channel_id=2, replica_groups=mesh['seq'=128,'fsdp'=4] {'seq'}, use_global_device_ids=true, to_apply=%add.1 | all-reduce | flops 1024 | bytes 8192
  438.6 2.1 collective-permute-start.3
  443.9 4.6 collective-permute-start.6
  455.2 1.9 constant_dynamic-update-slice_fusion.14
  457.1 2.3 collective-permute-done.4
  460.3 8.2 %collective-permute-done.5 = bf16[1,128,2048]{2,1,0:T(8,128)(2,1)S(1)} collective-permute-done((bf16[1,128,2048]{2,1,0:T(8,128)(2,1)S(1)}, bf16[1,128,2048]{2,1,0:T(8,128)(2,1)S(1)}, u32[]{:S(2)}, u32[]{:S(2)}) %collective-permute-start.5) | collective-permute-done | bytes 524320 | tf_op jit(solution)/shard_map/ppermute | solution.py:23
  471.9 7.1 collective-permute-done.8
  479.8 4.7 gather_fusion
  484.5 3.0 copy.75
  491.6 21.2 %all-gather.4.cloned.1.call-done = f32[1024,16,128]{2,1,0:T(8,128)} async-done(((f32[8,16,128]{2,1,0:T(8,128)}), f32[1024,16,128]{2,1,0:T(8,128)}) %all-gather.4.cloned.1.call-update) | async-done | bytes 8388624 | tf_op jit(solution)/shard_map/all_gather | solution.py:33
  512.8 206.2 %while.14 = (s32[]{:T(128)}, f32[8,16,128]{2,1,0:T(8,128)S(1)}, s32[]{:T(128)}, f32[128,8]{1,0:T(8,128)}, f32[128,8,16,128]{3,2,1,0:T(8,128)}, /*index=5*/s32[]{:T(128)}, s32[]{:T(128)}) while((s32[]{:T(128)}, f32[8,16,128]{2,1,0:T(8,128)S(1)}, s32[]{:T(128)}, f32[128,8]{1,0:T(8,128)}, f32[128,8,16,128]{3,2,1,0:T(8,128)}, ...), condition=%wide.region_6.7_spmd.clone, body=%wide.region_5.6_spmd.clone.sunk | while | flops 65540 | bytes 196817 | solution.py:42
  (366 shorter events, 234.2 us)
Async XLA Ops:
  6.5 162.0 %copy-start = (bf16[1,128,2048]{2,1,0:T(8,128)(2,1)S(1)}, bf16[1,128,2048]{2,1,0:T(8,128)(2,1)}, u32[]{:S(2)}) copy-start(bf16[1,128,2048]{2,1,0:T(8,128)(2,1)} %param.8) | copy-start | bytes 1572868
  6.5 83.1 %copy-start.16 = (f32[1,8,128]{2,1,0:T(8,128)S(1)}, f32[1,8,128]{2,1,0:T(8,128)}, u32[]{:S(2)}) copy-start(f32[1,8,128]{2,1,0:T(8,128)} %param.12) | copy-start | bytes 12292
  6.5 445.8 %all-reduce.4.cloned.1.call-start = ((), (), s32[]{:S(2)}) async-start(), calls=%async_computation | async-start | bytes 524288 | tf_op jit(solution)/shard_map/psum | solution.py:28
  11.3 67.4 %collective-permute-start = (bf16[2048,3,256]{0,2,1:T(8,128)(2,1)}, bf16[2048,3,256]{0,2,1:T(8,128)(2,1)}, u32[]{:S(2)}, u32[]{:S(2)}) collective-permute-start(bf16[2048,3,256]{0,2,1:T(8,128)(2,1)} %copy.47), channel_id=1, source_target_pairs={{0,1},{1,2},{2,3},{3,0},{4,5},{5,6},{6,7},{7,4},{8,9},{9,10},{10,1... | collective-permute-start | bytes 9437192 | tf_op jit(solution)/shard_map/ppermute | solution.py:70
  78.7 74.6 %collective-permute-start.1 = (bf16[2048,3,256]{0,2,1:T(8,128)(2,1)}, bf16[2048,3,256]{0,2,1:T(8,128)(2,1)}, u32[]{:S(2)}, u32[]{:S(2)}) collective-permute-start(bf16[2048,3,256]{0,2,1:T(8,128)(2,1)} %collective-permute-done), channel_id=1, source_target_pairs={{0,1},{1,2},{2,3},{3,0},{4,5},{5,6},{6,7},{7,4},{8,9},{9,10},{10,1... | collective-permute-start | bytes 9437192 | tf_op jit(solution)/shard_map/ppermute | solution.py:70
  85.4 73.5 %collective-permute-start.2 = (bf16[2048,3,256]{0,2,1:T(8,128)(2,1)}, bf16[2048,3,256]{0,2,1:T(8,128)(2,1)}, u32[]{:S(2)}, u32[]{:S(2)}) collective-permute-start(bf16[2048,3,256]{0,2,1:T(8,128)(2,1)} %copy.47), channel_id=1, source_target_pairs={{0,3},{1,0},{2,1},{3,2},{4,7},{5,4},{6,5},{7,6},{8,11},{9,8},{10,9... | collective-permute-start | bytes 9437192 | tf_op jit(solution)/shard_map/ppermute | solution.py:73
  172.1 271.8 %copy-start.3 = (bf16[1,128,1,1024]{1,3,2,0:T(8,128)(2,1)}, bf16[1,128,1,1024]{1,3,2,0:T(8,128)(2,1)S(1)}, u32[]{:S(2)}) copy-start(bf16[1,128,1,1024]{1,3,2,0:T(8,128)(2,1)S(1)} %get-tuple-element.132) | copy-start | bytes 786436
  173.2 339.6 %all-gather.4.cloned.1.call-start = ((), (), s32[]{:S(2)}) async-start(), calls=%async_computation.1 | async-start | bytes 8454144 | tf_op jit(solution)/shard_map/all_gather | solution.py:33
  173.5 276.4 %copy-start.8 = (f32[8,128,16]{1,2,0:T(8,128)}, f32[8,128,16]{1,2,0:T(8,128)S(1)}, u32[]{:S(2)}) copy-start(f32[8,128,16]{1,2,0:T(8,128)S(1)} %fusion.51) | copy-start | bytes 196612
  438.6 15.1 %collective-permute-start.3 = (bf16[1,128,2048]{2,1,0:T(8,128)(2,1)S(1)}, bf16[1,128,2048]{2,1,0:T(8,128)(2,1)}, u32[]{:S(2)}, u32[]{:S(2)}) collective-permute-start(bf16[1,128,2048]{2,1,0:T(8,128)(2,1)S(1)} %copy.54), channel_id=1, source_target_pairs={{0,12},{4,16},{8,20},{12,24},{16,28},{20,32},{24,36},{28,40},{32,4... | collective-permute-start | bytes 1572872 | tf_op jit(solution)/shard_map/ppermute | solution.py:23
  440.7 18.7 %collective-permute-start.4 = (bf16[1,128,2048]{2,1,0:T(8,128)(2,1)S(1)}, bf16[1,128,2048]{2,1,0:T(8,128)(2,1)S(1)}, u32[]{:S(2)}, u32[]{:S(2)}) collective-permute-start(bf16[1,128,2048]{2,1,0:T(8,128)(2,1)S(1)} %copy.54), channel_id=1, source_target_pairs={{0,8},{4,12},{8,16},{12,20},{16,24},{20,28},{24,32},{28,36},{32,40... | collective-permute-start | bytes 1572872 | tf_op jit(solution)/shard_map/ppermute | solution.py:23
  442.0 26.5 %collective-permute-start.5 = (bf16[1,128,2048]{2,1,0:T(8,128)(2,1)S(1)}, bf16[1,128,2048]{2,1,0:T(8,128)(2,1)S(1)}, u32[]{:S(2)}, u32[]{:S(2)}) collective-permute-start(bf16[1,128,2048]{2,1,0:T(8,128)(2,1)S(1)} %copy.54), channel_id=1, source_target_pairs={{0,4},{4,8},{8,12},{12,16},{16,20},{20,24},{24,28},{28,32},{32,36}... | collective-permute-start | bytes 1572872 | tf_op jit(solution)/shard_map/ppermute | solution.py:23
  443.9 26.2 %collective-permute-start.6 = (bf16[1,128,2048]{2,1,0:T(8,128)(2,1)S(1)}, bf16[1,128,2048]{2,1,0:T(8,128)(2,1)S(1)}, u32[]{:S(2)}, u32[]{:S(2)}) collective-permute-start(bf16[1,128,2048]{2,1,0:T(8,128)(2,1)S(1)} %copy.54), channel_id=1, source_target_pairs={{4,0},{8,4},{12,8},{16,12},{20,16},{24,20},{28,24},{32,28},{36,32}... | collective-permute-start | bytes 1572872 | tf_op jit(solution)/shard_map/ppermute | solution.py:23
  448.5 22.5 %collective-permute-start.7 = (bf16[1,128,2048]{2,1,0:T(8,128)(2,1)S(1)}, bf16[1,128,2048]{2,1,0:T(8,128)(2,1)S(1)}, u32[]{:S(2)}, u32[]{:S(2)}) collective-permute-start(bf16[1,128,2048]{2,1,0:T(8,128)(2,1)S(1)} %copy.54), channel_id=1, source_target_pairs={{8,0},{12,4},{16,8},{20,12},{24,16},{28,20},{32,24},{36,28},{40,32... | collective-permute-start | bytes 1572872 | tf_op jit(solution)/shard_map/ppermute | solution.py:23
  453.7 25.2 %collective-permute-start.8 = (bf16[1,128,2048]{2,1,0:T(8,128)(2,1)S(1)}, bf16[1,128,2048]{2,1,0:T(8,128)(2,1)S(1)}, u32[]{:S(2)}, u32[]{:S(2)}) collective-permute-start(bf16[1,128,2048]{2,1,0:T(8,128)(2,1)S(1)} %copy.54), channel_id=1, source_target_pairs={{12,0},{16,4},{20,8},{24,12},{28,16},{32,20},{36,24},{40,28},{44,3... | collective-permute-start | bytes 1572872 | tf_op jit(solution)/shard_map/ppermute | solution.py:23
  484.5 3.0 copy-start.12
  490.3 228.7 %copy-start.6 = (f32[8,128,16]{1,2,0:T(8,128)S(1)}, f32[8,128,16]{1,2,0:T(8,128)}, u32[]{:S(2)}) copy-start(f32[8,128,16]{1,2,0:T(8,128)} %get-tuple-element.140) | copy-start | bytes 196612
  490.3 228.7 %copy-start.11 = (f32[8,128]{1,0:T(8,128)S(1)}, f32[8,128]{1,0:T(8,128)}, u32[]{:S(2)}) copy-start(f32[8,128]{1,0:T(8,128)} %get-tuple-element.139) | copy-start | bytes 12292
  490.8 228.9 %copy-start.4 = (bf16[1,128,1,1024]{1,3,2,0:T(8,128)(2,1)S(1)}, bf16[1,128,1,1024]{1,3,2,0:T(8,128)(2,1)}, u32[]{:S(2)}) copy-start(bf16[1,128,1,1024]{1,3,2,0:T(8,128)(2,1)} %copy-done.3) | copy-start | bytes 786436
  490.8 228.9 %copy-start.9 = (f32[8,128,16]{1,2,0:T(8,128)S(1)}, f32[8,128,16]{1,2,0:T(8,128)}, u32[]{:S(2)}) copy-start(f32[8,128,16]{1,2,0:T(8,128)} %copy-done.8) | copy-start | bytes 196612
  490.8 228.9 %copy-start.10 = (pred[128,128]{1,0:T(8,128)(4,1)S(1)}, pred[128,128]{1,0:T(8,128)(4,1)}, u32[]{:S(2)}) copy-start(pred[128,128]{1,0:T(8,128)(4,1)} %iota_compare_fusion) | copy-start | bytes 49156
  490.8 228.9 %copy-start.18 = (f32[8,128]{1,0:T(8,128)S(1)}, f32[8,128]{1,0:T(8,128)}, u32[]{:S(2)}) copy-start(f32[8,128]{1,0:T(8,128)} %copy-done.17) | copy-start | bytes 12292
  491.0 229.2 %copy-start.14 = (f32[1024]{0:T(1024)S(1)}, f32[1024]{0:T(1024)}, u32[]{:S(2)}) copy-start(f32[1024]{0:T(1024)} %param.11) | copy-start | bytes 12292
  491.3 230.0 %copy-start.1 = (bf16[1,128,2048]{2,1,0:T(8,128)(2,1)S(1)}, bf16[1,128,2048]{2,1,0:T(8,128)(2,1)}, u32[]{:S(2)}) copy-start(bf16[1,128,2048]{2,1,0:T(8,128)(2,1)} %param.8) | copy-start | bytes 1572868
  (6 other events, 9.3 us)
Sparse Core Ops, SparseCore 0:
  173.4 195.4 all-reduce.3
  372.0 140.7 all-gather.3
